TPU v7x, 32 devices: a whole 2x2x4 slice. The times are simulated.
32 devices in a mesh: samples: 2 (over x), brick: 16 (over z, y, core).
Axes of the slice: x: 2, y: 2, z: 4, core: 2. Of those that a mesh axis runs over, the one named last changes fastest.
Arguments:
- source: float32 [128, 128, 256], P(('samples', 'brick')), parts along dimension 0, may hold values from -6 to 6
- guess: float32 [128, 128, 256], P(('samples', 'brick')), parts along dimension 0, may hold values from -6 to 6
- log_perm: float32 [128, 128, 256], P(('samples', 'brick')), parts along dimension 0, may hold values from -3 to 3
- owner: int32 [16], replicated, may hold values from 0 to 15, each once
Outputs:
- corrected: float32 [128, 128, 256], P(('samples', 'brick')), parts along dimension 0
- coarse_held: float32 [32, 2048], P(('samples', 'brick')), parts along dimension 0
There are 2 independent parts, one for each index of `samples`. A program takes and returns all parts, laid end to end along the dimension named above; an argument that names none is the same for every part. Nothing has to cross between parts.
Inputs may be any that keep to these rules, and one draw needn't show every extreme that they name: `owner`: each brick index appears exactly once.
All inputs are finite; a program needn't handle non-finite values.
Results may differ from a plain program's by a relative error of at most 0.00005.
Values sent between devices are 32-bit elements; how exact they have to be, the bound alone decides.
A program may use at most 64 MiB of HBM per device.

v0:
```python
import jax
import jax.numpy as jnp
from jax import lax
from jax.sharding import PartitionSpec as P

NU = 2
SWEEPS = 8


relax_weight = 0.8


def with_halo(block, sides, width):
    for axis, dim in sides:
        count = lax.axis_size(axis)
        forward = [(i, i + 1) for i in range(count - 1)]
        backward = [(target, source) for source, target in forward]
        low = lax.ppermute(
            lax.slice_in_dim(block, block.shape[dim] - width, None, axis=dim), axis, forward
        )
        high = lax.ppermute(lax.slice_in_dim(block, 0, width, axis=dim), axis, backward)
        block = jnp.concatenate([low, block, high], axis=dim)
    return block


def prolong_matrix(n_fine):
    fine_idx = jnp.arange(n_fine)[:, None]
    coarse_idx = jnp.arange(n_fine // 4)[None, :]
    base = fine_idx // 4
    offset = fine_idx % 4
    weight_own = jnp.where((offset == 0) | (offset == 3), 0.625, 0.875).astype(jnp.float32)
    side = jnp.where(offset < 2, -1, 1)
    own = jnp.where(coarse_idx == base, weight_own, 0.0)
    other = jnp.where(coarse_idx == base + side, 1.0 - weight_own, 0.0)
    return own + other


def local_prolong(planes):
    fine_idx = jnp.arange(planes)[:, None]
    coarse_idx = jnp.arange(planes // 4 + 2)[None, :]
    base = fine_idx // 4 + 1
    offset = fine_idx % 4
    weight_own = jnp.where((offset == 0) | (offset == 3), 0.625, 0.875).astype(jnp.float32)
    side = jnp.where(offset < 2, -1, 1)
    own = jnp.where(coarse_idx == base, weight_own, 0.0)
    other = jnp.where(coarse_idx == base + side, 1.0 - weight_own, 0.0)
    return own + other


def stencil(u_ext, k_ext):
    padded = jnp.pad(u_ext, ((0, 0), (1, 1), (1, 1)))
    kpad = jnp.pad(k_ext, ((0, 0), (1, 1), (1, 1)))
    center = padded[1:-1, 1:-1, 1:-1]
    kcen = kpad[1:-1, 1:-1, 1:-1]
    pairs = [
        (padded[:-2, 1:-1, 1:-1], kpad[:-2, 1:-1, 1:-1]),
        (padded[2:, 1:-1, 1:-1], kpad[2:, 1:-1, 1:-1]),
        (padded[1:-1, :-2, 1:-1], kpad[1:-1, :-2, 1:-1]),
        (padded[1:-1, 2:, 1:-1], kpad[1:-1, 2:, 1:-1]),
        (padded[1:-1, 1:-1, :-2], kpad[1:-1, 1:-1, :-2]),
        (padded[1:-1, 1:-1, 2:], kpad[1:-1, 1:-1, 2:]),
    ]
    diagonal = jnp.zeros_like(center)
    nearby = jnp.zeros_like(center)
    for value, kval in pairs:
        face = 0.5 * (kcen + kval)
        diagonal = diagonal + face
        nearby = nearby + face * value
    return (diagonal * center - nearby, diagonal)


def coarse_apply(field, coeff, zcount):
    columns = field.shape[1]
    zpos = jnp.arange(columns) % zcount
    low_ok = (zpos > 0)[None, :]
    high_ok = (zpos < zcount - 1)[None, :]

    def rows_down(a):
        return jnp.pad(a[:-1], ((1, 0), (0, 0)))

    def rows_up(a):
        return jnp.pad(a[1:], ((0, 1), (0, 0)))

    def cols_down(a, width):
        return jnp.pad(a[:, :-width], ((0, 0), (width, 0)))

    def cols_up(a, width):
        return jnp.pad(a[:, width:], ((0, 0), (0, width)))

    pairs = [
        (rows_down(field), rows_down(coeff)),
        (rows_up(field), rows_up(coeff)),
        (cols_down(field, zcount), cols_down(coeff, zcount)),
        (cols_up(field, zcount), cols_up(coeff, zcount)),
        (jnp.where(low_ok, cols_down(field, 1), 0.0), jnp.where(low_ok, cols_down(coeff, 1), 0.0)),
        (jnp.where(high_ok, cols_up(field, 1), 0.0), jnp.where(high_ok, cols_up(coeff, 1), 0.0)),
    ]
    diagonal = jnp.zeros_like(field)
    nearby = jnp.zeros_like(field)
    for value, kval in pairs:
        face = 0.5 * (coeff + kval)
        diagonal = diagonal + face
        nearby = nearby + face * value
    return (diagonal * field - nearby, diagonal)


def faces(field):
    return with_halo(field, (("brick", 0),), 1)


def local(source, guess, log_perm, owner):
    hp = lax.Precision.HIGHEST
    planes, ny_local, nz_local = source.shape
    cpd = planes // 4
    cyc = ny_local // 4
    czc = nz_local // 4
    cells = cyc * czc
    count = lax.axis_size("brick")
    device = lax.axis_index("brick")
    perm = jnp.exp(log_perm)
    k_ext = with_halo(perm, (("brick", 0),), 1)
    smooth = guess
    for sweep in range(NU):
        image, diagonal = stencil(faces(smooth), k_ext)
        smooth = smooth + relax_weight * (source - image) / diagonal
    image, diagonal = stencil(faces(smooth), k_ext)
    resid = source - image
    py = prolong_matrix(ny_local)
    pz = prolong_matrix(nz_local)
    p_local = local_prolong(planes)
    step_one = jnp.einsum("xyz,yY->xYz", resid, py, precision=hp)
    step_two = jnp.einsum("xYz,zZ->xYZ", step_one, pz, precision=hp)
    partial_value = jnp.einsum("xYZ,xj->jYZ", step_two, p_local, precision=hp) * (1.0 / 64.0)
    partial_value = partial_value.reshape(cpd + 2, cells)
    coarse_own = perm.reshape(cpd, 4, cyc, 4, czc, 4).sum(axis=(1, 3, 5)) * (1.0 / 64.0)
    coarse_own = coarse_own.reshape(cpd, cells)
    middle = partial_value[1 : cpd + 1]
    has_prev = device > 0
    has_next = device < count - 1
    filler = jnp.zeros((cpd - 1, cells), jnp.float32)
    lower_part = jnp.concatenate([filler, partial_value[0:1]], axis=0)
    upper_part = jnp.concatenate([partial_value[cpd + 1 :], filler], axis=0)
    block_ids = jnp.arange(count)[:, None, None]
    self_dest = jnp.take(owner, device)
    prev_dest = jnp.take(owner, jnp.clip(device - 1, 0, count - 1))
    next_dest = jnp.take(owner, jnp.clip(device + 1, 0, count - 1))
    buffer = jnp.where(block_ids == self_dest, middle[None], 0.0)
    buffer = buffer + jnp.where((block_ids == prev_dest) & has_prev, lower_part[None], 0.0)
    buffer = buffer + jnp.where((block_ids == next_dest) & has_next, upper_part[None], 0.0)
    held_rhs = lax.psum_scatter(buffer, "brick", scatter_dimension=0, tiled=True)
    gathered_rhs, coarse_perm = (
        lax.all_gather(held_rhs.reshape(cpd, cells), "brick", axis=0, tiled=True),
        lax.all_gather(coarse_own, "brick", axis=0, tiled=True),
    )
    coarse_rhs = jnp.take(gathered_rhs.reshape(count, cpd, cells), owner, axis=0).reshape(
        count * cpd, cells
    )
    coarse = jnp.zeros_like(coarse_rhs)
    for sweep in range(SWEEPS):
        image, diagonal = coarse_apply(coarse, coarse_perm, czc)
        coarse = coarse + relax_weight * (coarse_rhs - image * (1.0 / 16.0)) / (
            diagonal * (1.0 / 16.0)
        )
    coarse_pad = jnp.pad(coarse, ((1, 1), (0, 0)))
    near_planes = lax.dynamic_slice_in_dim(coarse_pad, device * cpd, cpd + 2, 0).reshape(
        cpd + 2, cyc, czc
    )
    back_one = jnp.einsum("jYZ,xj->xYZ", near_planes, p_local, precision=hp)
    back_two = jnp.einsum("xYZ,yY->xyZ", back_one, py, precision=hp)
    correction = jnp.einsum("xyZ,zZ->xyz", back_two, pz, precision=hp)
    corrected = smooth + correction
    my_block = jnp.sum(jnp.where(owner == device, jnp.arange(count), 0))
    coarse_held = lax.dynamic_slice_in_dim(coarse, my_block * cpd, cpd, 0)
    return (corrected, coarse_held)


def solution(mesh):
    placed = (
        P(("samples", "brick"), None, None),
        P(("samples", "brick"), None, None),
        P(("samples", "brick"), None, None),
        P(),
    )
    return jax.shard_map(
        local,
        mesh=mesh,
        in_specs=placed,
        out_specs=(P(("samples", "brick"), None, None), P(("samples", "brick"), None)),
        check_vma=False,
    )
```

profile of v0, /device:TPU:0, one launch (start us, length us, event | category | flops | bytes accessed | tf_op | source)
XLA Modules:
  0.0 212.1 jit_solution(589605700976618355)
XLA Ops:
  7.2 1.2 exponential_reduce_fusion
  8.4 2.4 %collective-permute-start = (f32[1,128,256]{2,1,0:T(8,128)S(1)}, f32[1,128,256]{2,1,0:T(8,128)S(1)}, u32[]{:S(2)}, u32[]{:S(2)}) collective-permute-start(f32[1,128,256]{2,1,0:T(8,128)S(1)} %get-tuple-element.52), channel_id=1, source_target_pairs={{0,1},{1,2},{2,3},{3,4},{4,5},{5,6},{6,7},{7,8},{8,9},{9,10},{10,1... | collective-permute-start | bytes 393224 | tf_op jit(solution)/shard_map/ppermute | solution.py:18
  10.8 1.3 collective-permute-start.1
  12.1 5.8 %collective-permute-start.2 = (f32[1,128,256]{2,1,0:T(8,128)S(1)}, f32[1,128,256]{2,1,0:T(8,128)}, u32[]{:S(2)}, u32[]{:S(2)}) collective-permute-start(f32[1,128,256]{2,1,0:T(8,128)S(1)} %get-tuple-element.53), channel_id=1, source_target_pairs={{0,1},{1,2},{2,3},{3,4},{4,5},{5,6},{6,7},{7,8},{8,9},{9,10},{10,1... | collective-permute-start | bytes 393224 | tf_op jit(solution)/shard_map/ppermute | solution.py:18
  18.0 1.3 collective-permute-start.3
  19.3 5.7 %reduce_sum.26 = f32[32,4,64,4]{3,2,1,0:T(8,128)} reshape(f32[128,256]{1,0:T(8,128)S(1)} %get-tuple-element.45) | data formatting | bytes 262144 | tf_op jit(solution)/shard_map/reduce_sum | solution.py:135
  25.0 2.5 %reduce_sum.27 = f32[32,64]{1,0:T(8,128)S(1)} reduce(f32[32,4,64,4]{3,2,1,0:T(8,128)} %reduce_sum.26, f32[]{:T(128)} %constant.184.clone.1), dimensions={1,3}, to_apply=%region_2.3 | reduce | flops 30720 | bytes 139268 | tf_op jit(solution)/shard_map/reduce_sum | solution.py:135
  27.6 23.8 %all-gather.1 = f32[16,1,2048]{2,1,0:T(1,128)S(1)} all-gather(f32[1,1,2048]{2,1,0:T(1,128)S(1)} %reshape.582), channel_id=1, replica_groups=mesh['samples'=2,'brick'=16] {'brick'}, dimensions={0}, use_global_device_ids=true | all-gather | bytes 139264 | tf_op jit(solution)/shard_map/all_gather | solution.py:153
  52.4 0.8 fusion.149
  53.8 0.8 copy_bitcast_fusion
  57.8 1.3 select_maximum_fusion.6
  59.8 1.3 select_maximum_fusion.4
  61.2 2.2 %fusion.37 = f32[4,128,256]{2,1,0:T(8,128)S(1)} fusion(f32[4,128,256]{2,1,0:T(8,128)S(1)} %copy-done, f32[4,128,256]{2,1,0:T(8,128)S(1)} %copy-done.1, f32[6,130,258]{2,1,0:T(8,128)S(1)} %select_maximum_fusion.4, f32[1,128,256]{2,1,0:T(8,128)} %copy-done.11, f32[1,128,256]{2,1,0:T(8,128)} %collective-permute-done.2, ...), kind=kLoop, calls=%fused_computation.61 | loop fusion | flops 4980736 | bytes 6815744 | tf_op jit(solution)/shard_map/add | solution.py:125
  63.4 2.3 %collective-permute-start.4 = (f32[1,128,256]{2,1,0:T(8,128)S(1)}, f32[1,128,256]{2,1,0:T(8,128)S(1)}, u32[]{:S(2)}, u32[]{:S(2)}) collective-permute-start(f32[1,128,256]{2,1,0:T(8,128)S(1)} %get-tuple-element.49), channel_id=1, source_target_pairs={{0,1},{1,2},{2,3},{3,4},{4,5},{5,6},{6,7},{7,8},{8,9},{9,10},{10,1... | collective-permute-start | bytes 393224 | tf_op jit(solution)/shard_map/ppermute | solution.py:18
  65.6 1.3 collective-permute-start.5
  67.5 1.3 collective-permute-done.5
  70.0 2.2 %fusion.25 = f32[4,128,256]{2,1,0:T(8,128)S(1)} fusion(f32[4,128,256]{2,1,0:T(8,128)S(1)} %fusion.37, f32[4,128,256]{2,1,0:T(8,128)S(1)} %copy-done.1, f32[6,130,258]{2,1,0:T(8,128)S(1)} %select_maximum_fusion.2, f32[1,128,256]{2,1,0:T(8,128)} %copy-done.13, f32[1,128,256]{2,1,0:T(8,128)} %copy-done.12, f32[4,128,256]{2,1,0:T(8,128)S(1)} %get-tuple-element.46, ...), kind=kLoop, calls=%fused_computation.43 | loop fusion | flops 4980736 | bytes 6815744 | tf_op jit(solution)/shard_map/add | solution.py:125
  72.9 5.0 %collective-permute-start.6 = (f32[1,128,256]{2,1,0:T(8,128)}, f32[1,128,256]{2,1,0:T(8,128)S(1)}, u32[]{:S(2)}, u32[]{:S(2)}) collective-permute-start(f32[1,128,256]{2,1,0:T(8,128)} %get-tuple-element.47), channel_id=1, source_target_pairs={{0,1},{1,2},{2,3},{3,4},{4,5},{5,6},{6,7},{7,8},{8,9},{9,10},{10,1... | collective-permute-start | bytes 393224 | tf_op jit(solution)/shard_map/ppermute | solution.py:18
  77.9 1.3 collective-permute-start.7
  82.3 2.4 %convolution_bitcast_fusion = f32[4,32,256]{2,1,0:T(8,128)S(1)} fusion(f32[4,128,256]{2,1,0:T(8,128)S(1)} %copy-done.1, f32[6,130,258]{2,1,0:T(8,128)S(1)} %select_maximum_fusion, f32[1,128,256]{2,1,0:T(8,128)S(1)} %collective-permute-done.7, f32[4,128,256]{2,1,0:T(8,128)S(1)} %fusion.25, f32[1,128,256]{2,1,0:T(8,128)S(1)} %collective-permute-done.6, ...), kind=kOutput, calls=%fused_computation.17 | convolution fusion | flops 54939648 | bytes 6424576 | tf_op jit(solution)/shard_map/xyz,yY->xYz/dot_general | solution.py:131
  86.6 87.5 %all-reduce.62.cloned.1.call-done = f32[16,1,2048]{2,0,1:T(8,128)} async-done(((f32[16,1,2048]{2,0,1:T(8,128)}), f32[16,1,2048]{2,0,1:T(8,128)}) %all-reduce.62.cloned.1.call-update) | async-done | bytes 131088
  174.0 1.4 dynamic-slice_bitcast_fusion
  175.4 22.6 %all-gather = f32[16,1,2048]{2,1,0:T(1,128)S(1)} all-gather(f32[1,1,2048]{2,1,0:T(1,128)S(1)} %dynamic-slice_bitcast_fusion), channel_id=2, replica_groups=mesh['samples'=2,'brick'=16] {'brick'}, dimensions={0}, use_global_device_ids=true | all-gather | bytes 139264 | tf_op jit(solution)/shard_map/all_gather | solution.py:152
  203.2 1.4 convolution_add_fusion
  (116 shorter events, 14.5 us)
Async XLA Ops:
  7.2 4.9 %copy-start = (f32[4,128,256]{2,1,0:T(8,128)S(1)}, f32[4,128,256]{2,1,0:T(8,128)}, u32[]{:S(2)}) copy-start(f32[4,128,256]{2,1,0:T(8,128)} %param.5) | copy-start | bytes 1572868
  7.2 166.9 %all-reduce.62.cloned.1.call-start = ((), (), s32[]{:S(2)}) async-start(), calls=%async_computation | async-start | bytes 262144
  8.4 48.7 %collective-permute-start = (f32[1,128,256]{2,1,0:T(8,128)S(1)}, f32[1,128,256]{2,1,0:T(8,128)S(1)}, u32[]{:S(2)}, u32[]{:S(2)}) collective-permute-start(f32[1,128,256]{2,1,0:T(8,128)S(1)} %get-tuple-element.52), channel_id=1, source_target_pairs={{0,1},{1,2},{2,3},{3,4},{4,5},{5,6},{6,7},{7,8},{8,9},{9,10},{10,1... | collective-permute-start | bytes 393224 | tf_op jit(solution)/shard_map/ppermute | solution.py:18
  10.8 46.4 %collective-permute-start.1 = (f32[1,128,256]{2,1,0:T(8,128)S(1)}, f32[1,128,256]{2,1,0:T(8,128)}, u32[]{:S(2)}, u32[]{:S(2)}) collective-permute-start(f32[1,128,256]{2,1,0:T(8,128)S(1)} %get-tuple-element.51), channel_id=1, source_target_pairs={{1,0},{2,1},{3,2},{4,3},{5,4},{6,5},{7,6},{8,7},{9,8},{10,9},{11,1... | collective-permute-start | bytes 393224 | tf_op jit(solution)/shard_map/ppermute | solution.py:21
  12.1 47.0 %collective-permute-start.2 = (f32[1,128,256]{2,1,0:T(8,128)S(1)}, f32[1,128,256]{2,1,0:T(8,128)}, u32[]{:S(2)}, u32[]{:S(2)}) collective-permute-start(f32[1,128,256]{2,1,0:T(8,128)S(1)} %get-tuple-element.53), channel_id=1, source_target_pairs={{0,1},{1,2},{2,3},{3,4},{4,5},{5,6},{6,7},{7,8},{8,9},{9,10},{10,1... | collective-permute-start | bytes 393224 | tf_op jit(solution)/shard_map/ppermute | solution.py:18
  18.0 41.2 %collective-permute-start.3 = (f32[1,128,256]{2,1,0:T(8,128)S(1)}, f32[1,128,256]{2,1,0:T(8,128)S(1)}, u32[]{:S(2)}, u32[]{:S(2)}) collective-permute-start(f32[1,128,256]{2,1,0:T(8,128)S(1)} %get-tuple-element.54), channel_id=1, source_target_pairs={{1,0},{2,1},{3,2},{4,3},{5,4},{6,5},{7,6},{8,7},{9,8},{10,9},{11,1... | collective-permute-start | bytes 393224 | tf_op jit(solution)/shard_map/ppermute | solution.py:21
  27.5 25.6 %copy-start.14 = (s32[16]{0:T(128)S(1)}, s32[16]{0:T(128)}, u32[]{:S(2)}) copy-start(s32[16]{0:T(128)} %param.7) | copy-start | bytes 196
  59.1 2.0 copy-start.1
  59.1 2.0 copy-start.3
  63.4 4.1 %collective-permute-start.4 = (f32[1,128,256]{2,1,0:T(8,128)S(1)}, f32[1,128,256]{2,1,0:T(8,128)S(1)}, u32[]{:S(2)}, u32[]{:S(2)}) collective-permute-start(f32[1,128,256]{2,1,0:T(8,128)S(1)} %get-tuple-element.49), channel_id=1, source_target_pairs={{0,1},{1,2},{2,3},{3,4},{4,5},{5,6},{6,7},{7,8},{8,9},{9,10},{10,1... | collective-permute-start | bytes 393224 | tf_op jit(solution)/shard_map/ppermute | solution.py:18
  65.6 3.2 %collective-permute-start.5 = (f32[1,128,256]{2,1,0:T(8,128)S(1)}, f32[1,128,256]{2,1,0:T(8,128)S(1)}, u32[]{:S(2)}, u32[]{:S(2)}) collective-permute-start(f32[1,128,256]{2,1,0:T(8,128)S(1)} %get-tuple-element.50), channel_id=1, source_target_pairs={{1,0},{2,1},{3,2},{4,3},{5,4},{6,5},{7,6},{8,7},{9,8},{10,9},{11,1... | collective-permute-start | bytes 393224 | tf_op jit(solution)/shard_map/ppermute | solution.py:21
  67.5 1.4 copy-start.12
  70.0 10.6 %copy-start.15 = (u32[32]{0:T(128)S(1)}, u32[32]{0:T(128)}, u32[]{:S(2)}) copy-start(u32[32]{0:T(128)} %constant.395) | copy-start | bytes 388
  72.2 10.0 %copy-start.4 = (f32[1,128,256]{2,1,0:T(8,128)S(1)}, f32[1,128,256]{2,1,0:T(8,128)}, u32[]{:S(2)}) copy-start(f32[1,128,256]{2,1,0:T(8,128)} %copy-done.2) | copy-start | bytes 393220
  72.9 8.9 %collective-permute-start.6 = (f32[1,128,256]{2,1,0:T(8,128)}, f32[1,128,256]{2,1,0:T(8,128)S(1)}, u32[]{:S(2)}, u32[]{:S(2)}) collective-permute-start(f32[1,128,256]{2,1,0:T(8,128)} %get-tuple-element.47), channel_id=1, source_target_pairs={{0,1},{1,2},{2,3},{3,4},{4,5},{5,6},{6,7},{7,8},{8,9},{9,10},{10,1... | collective-permute-start | bytes 393224 | tf_op jit(solution)/shard_map/ppermute | solution.py:18
  77.9 4.0 %collective-permute-start.7 = (f32[1,128,256]{2,1,0:T(8,128)S(1)}, f32[1,128,256]{2,1,0:T(8,128)S(1)}, u32[]{:S(2)}, u32[]{:S(2)}) collective-permute-start(f32[1,128,256]{2,1,0:T(8,128)S(1)} %get-tuple-element.48), channel_id=1, source_target_pairs={{1,0},{2,1},{3,2},{4,3},{5,4},{6,5},{7,6},{8,7},{9,8},{10,9},{11,1... | collective-permute-start | bytes 393224 | tf_op jit(solution)/shard_map/ppermute | solution.py:21
  82.2 2.7 %copy-start.16 = (s32[4]{0:T(128)S(1)}, s32[4]{0:T(128)}, u32[]{:S(2)}) copy-start(s32[4]{0:T(128)} %get-tuple-element.114) | copy-start | bytes 52
  82.3 2.7 %copy-start.17 = (s32[4]{0:T(128)S(1)}, s32[4]{0:T(128)}, u32[]{:S(2)}) copy-start(s32[4]{0:T(128)} %get-tuple-element.115) | copy-start | bytes 52
  85.3 113.4 %copy-start.5 = (f32[16,1984]{1,0:T(8,128)S(1)}, f32[16,1984]{1,0:T(8,128)}, u32[]{:S(2)}) copy-start(f32[16,1984]{1,0:T(8,128)} %get-tuple-element.99) | copy-start | bytes 380932
  85.4 113.4 %copy-start.6 = (f32[16,1984]{1,0:T(8,128)S(1)}, f32[16,1984]{1,0:T(8,128)}, u32[]{:S(2)}) copy-start(f32[16,1984]{1,0:T(8,128)} %get-tuple-element.100) | copy-start | bytes 380932
  85.4 113.4 %copy-start.7 = (f32[16,2047]{1,0:T(8,128)S(1)}, f32[16,2047]{1,0:T(8,128)}, u32[]{:S(2)}) copy-start(f32[16,2047]{1,0:T(8,128)} %get-tuple-element.97) | copy-start | bytes 393028
  85.4 113.4 %copy-start.8 = (f32[16,2047]{1,0:T(8,128)S(1)}, f32[16,2047]{1,0:T(8,128)}, u32[]{:S(2)}) copy-start(f32[16,2047]{1,0:T(8,128)} %get-tuple-element.98) | copy-start | bytes 393028
  85.4 113.4 %copy-start.9 = (f32[15,2048]{1,0:T(8,128)S(1)}, f32[15,2048]{1,0:T(8,128)}, u32[]{:S(2)}) copy-start(f32[15,2048]{1,0:T(8,128)} %get-tuple-element.122) | copy-start | bytes 368644
  85.4 113.4 %copy-start.10 = (f32[15,2048]{1,0:T(8,128)S(1)}, f32[15,2048]{1,0:T(8,128)}, u32[]{:S(2)}) copy-start(f32[15,2048]{1,0:T(8,128)} %get-tuple-element.123) | copy-start | bytes 368644
  (3 other events, 2.0 us)
Sparse Core Ops, SparseCore 0:
  86.7 87.3 all-reduce.61
where the time goes:
time: 213 us; the launch traced here: 212 us
  waiting for transfers between devices  88.9 us (42%)
  blocking collectives  46.4 us (22%)
  starting transfers between devices  20.6 us (10%)
  between operations  18.7 us (9%)
  local copies, waits for them, and re-layouts  16.8 us (8%)
  other arithmetic  15.6 us (7%)
  matrix products  5.18 us (2%)
    unnamed x2, waiting for transfers between devices  87.5 us
    all_gather x1, blocking collectives, local(): lax.all_gather(coarse_own, 'brick', axis=0, tiled=True)  23.8 us
    all_gather x1, blocking collectives, local(): lax.all_gather(held_rhs.reshape(cpd, cells), 'brick', axis=0, tiled=True)  22.6 us
    ppermute x4, starting transfers between devices, with_halo(): lax.ppermute(lax.slice_in_dim(block, block.shape[dim] - width, None, axis...  15.4 us
    reduce_sum x1, local copies, waits for them, and re-layouts, local(): perm.reshape(cpd, 4, cyc, 4, czc, 4).sum(axis=(1, 3, 5)) * (1.0 / 64.0)  5.67 us
    ppermute x4, starting transfers between devices, with_halo(): lax.ppermute(lax.slice_in_dim(block, 0, width, axis=dim), axis, backward)  5.16 us
    add x2, other arithmetic, local(): smooth = smooth + relax_weight * (source - image) / diagonal  4.4 us
  transfers between devices with their start and end apart: 9, of which 2 were waited for; matrix products, arithmetic and copies ran while one was open for 7% of the time, Pallas kernels for 0%

commit v1 on v0

v1 whole, which is shorter than its diff:
```python
import functools

import jax
import jax.numpy as jnp
import ml_dtypes
import numpy as np
from jax import lax
from jax.experimental import pallas as pl
from jax.experimental.pallas import tpu as pltpu
from jax.sharding import PartitionSpec as P

SWEEPS = 8
CHUNKS = 4
MESH = pl.DeviceIdType.MESH
F32 = jnp.float32
BF16 = jnp.bfloat16


def prolong_matrix(n_fine):
    i = np.arange(n_fine)[:, None]
    j = np.arange(n_fine // 4)[None, :]
    base, offset = i // 4, i % 4
    own = np.where((offset == 0) | (offset == 3), 0.625, 0.875)
    side = np.where(offset < 2, -1, 1)
    return np.where(j == base, own, 0.0) + np.where(j == base + side, 1.0 - own, 0.0)


def mean_matrix(n_fine):
    i = np.arange(n_fine)[:, None]
    j = np.arange(n_fine // 4)[None, :]
    return np.where(j == i // 4, 1.0, 0.0)


def even_odd(m):
    return np.concatenate([m[:, 0::2], m[:, 1::2]], axis=1)


def halves(m):
    zero = np.zeros_like(m)
    return np.stack([np.concatenate([m, zero], 1), np.concatenate([zero, m], 1)])


def split(x):
    hi = x.astype(BF16)
    return hi, (x - hi.astype(F32)).astype(BF16)


def dot(a, b):
    return jnp.dot(a, b, preferred_element_type=F32)


def to_coarse(y_mat, z_mat, x):
    hi, lo = split(x)
    a = dot(y_mat, hi) + dot(y_mat, lo)
    hi, lo = split(a)
    h = a.shape[0] // 2
    return (
        dot(hi[:h], z_mat[0]) + dot(lo[:h], z_mat[0]) + dot(hi[h:], z_mat[1]) + dot(lo[h:], z_mat[1])
    )


def smooth_kernel(
    n, ny, nz,
    source_hbm, guess_hbm, logq_hbm, ry, rz, my, mz,
    smooth, all_rhs, all_q,
    src, logq, K, U0, U1, U2, D, N, EK, X, H, own, part,
    local_sem, halo_send, halo_recv, part_send, part_recv, q_send, q_recv, r_send, r_recv,
):
    me = lax.axis_index("brick")
    R = ny // CHUNKS
    has = (me > 0, me < n - 1)
    peer_of = (me - 1, me + 1)

    loads = [
        pltpu.make_async_copy(logq_hbm, logq, local_sem.at[0]),
        pltpu.make_async_copy(guess_hbm, U0.at[pl.ds(1, 4), pl.ds(8, ny)], local_sem.at[1]),
        pltpu.make_async_copy(source_hbm, src, local_sem.at[2]),
    ]
    for copy in loads:
        copy.start()

    barrier = pltpu.get_barrier_semaphore()

    def greet(k, _):
        pl.semaphore_signal(
            barrier, inc=1, device_id={"brick": lax.rem(me + k, n)}, device_id_type=MESH
        )
        return 0

    lax.fori_loop(1, n, greet, 0)
    pl.semaphore_wait(barrier, n - 1)

    def halo(which, side, c):
        plane = 3 * side
        start = c * R if isinstance(c, int) else pl.multiple_of(c * R, R)
        rows = pl.ds(start, R)
        if which == 2:
            ref = U1.at[plane + 1, pl.ds(start + 8, R)]
        else:
            ref = (logq_hbm, guess_hbm)[which].at[plane, rows]
        return pltpu.make_async_remote_copy(
            src_ref=ref,
            dst_ref=H.at[which, 1 - side, rows],
            send_sem=halo_send.at[which, side, c],
            recv_sem=halo_recv.at[which, 1 - side, c],
            device_id={"brick": peer_of[side]},
            device_id_type=MESH,
        )

    def arrival(which, side, c):
        start = c * R if isinstance(c, int) else pl.multiple_of(c * R, R)
        ref = H.at[which, side, pl.ds(start, R)]
        return pltpu.make_async_remote_copy(
            src_ref=ref,
            dst_ref=ref,
            send_sem=halo_send.at[which, side, c],
            recv_sem=halo_recv.at[which, side, c],
            device_id={"brick": peer_of[side]},
            device_id_type=MESH,
        )

    for c in range(CHUNKS):
        for side in range(2):

            @pl.when(has[side])
            def _():
                halo(0, side, c).start()
                halo(1, side, c).start()

    zero_plane = jnp.zeros((ny + 16, nz), F32)
    zero_rows = jnp.zeros((8, nz), F32)
    for ref in (K, U0, U1, U2):
        ref[0] = zero_plane
        ref[5] = zero_plane
        for p in range(1, 5):
            ref[p, 0:8] = zero_rows
            ref[p, ny + 8 : ny + 16] = zero_rows

    lane = lax.broadcasted_iota(jnp.int32, (R, nz), 1)
    first, last = lane == 0, lane == nz - 1

    def yz(window):
        center = window[8 : R + 8]
        low = jnp.where(first, 0.0, pltpu.roll(center, 1, 1))
        high = jnp.where(last, 0.0, pltpu.roll(center, nz - 1, 1))
        return (window[7 : R + 7] + window[9 : R + 9]) + (low + high)

    loads[0].wait()

    def exps(i, _):
        p, start = i // CHUNKS, pl.multiple_of((i % CHUNKS) * R, R)
        K[p + 1, pl.ds(start + 8, R)] = jnp.exp(logq[p, pl.ds(start, R)])
        return 0

    lax.fori_loop(0, 4 * CHUNKS, exps, 0)
    loads[1].wait()
    loads[2].wait()

    def nearby(U, p, start):
        at = pl.ds(start + 8, R)
        window = pl.ds(start, R + 16)
        u, k = U[p + 1, window], K[p + 1, window]
        um, up, km, kp = U[p, at], U[p + 2, at], K[p, at], K[p + 2, at]
        su = yz(u) + (um + up)
        sku = yz(u * k) + (km * um + kp * up)
        q = k[8 : R + 8]
        return u[8 : R + 8], q, k, km + kp, 0.5 * (q * su + sku)

    def sweep_one(i, _):
        p, start = i // CHUNKS, pl.multiple_of((i % CHUNKS) * R, R)
        rows = pl.ds(start, R)
        u, q, k, kx, near = nearby(U0, p, start)
        d = 3.0 * q + 0.5 * (yz(k) + kx)
        total = src[p, rows] + near
        D[p, rows] = d
        N[p, rows] = total
        U1[p + 1, pl.ds(start + 8, R)] = 0.2 * u + 0.8 * total / d
        return 0

    lax.fori_loop(0, 4 * CHUNKS, sweep_one, 0)

    own[...] = to_coarse(
        my[...], mz, (K[1, 8 : ny + 8] + K[2, 8 : ny + 8]) + (K[3, 8 : ny + 8] + K[4, 8 : ny + 8])
    ) * (1.0 / 64.0)
    all_q[me] = own[...]

    def finish_one(c, _):
        start = pl.multiple_of(c * R, R)
        rows, at = pl.ds(start, R), pl.ds(start + 8, R)
        for side in range(2):
            p = 3 * side

            @pl.when(has[side])
            def _():
                arrival(0, side, c).wait_recv()
                arrival(1, side, c).wait_recv()
                q = K[p + 1, at]
                kh = jnp.exp(H[0, side, rows])
                EK[side, rows] = kh
                D[p, rows] = D[p, rows] + 0.5 * kh
                N[p, rows] = N[p, rows] + 0.5 * (q + kh) * H[1, side, rows]

            @pl.when(jnp.logical_not(has[side]))
            def _():
                EK[side, rows] = jnp.zeros((R, nz), F32)

            U1[p + 1, at] = 0.2 * U0[p + 1, at] + 0.8 * N[p, rows] / D[p, rows]

            @pl.when(has[side])
            def _():
                halo(2, side, c).start()

        return 0

    lax.fori_loop(0, CHUNKS, finish_one, 0)

    def spread(ref, k, send, recv):
        return pltpu.make_async_remote_copy(
            src_ref=ref.at[me],
            dst_ref=ref.at[me],
            send_sem=send.at[k],
            recv_sem=recv.at[me],
            device_id={"brick": lax.rem(me + k, n)},
            device_id_type=MESH,
        )

    def landed(ref, k, send, recv):
        who = lax.rem(me + k, n)
        return pltpu.make_async_remote_copy(
            src_ref=ref.at[who],
            dst_ref=ref.at[who],
            send_sem=send.at[k],
            recv_sem=recv.at[who],
            device_id={"brick": who},
            device_id_type=MESH,
        )

    def send_q(k, _):
        spread(all_q, k, q_send, q_recv).start()
        return 0

    lax.fori_loop(1, n, send_q, 0)

    def sweep_two(i, _):
        p, start = i // CHUNKS, pl.multiple_of((i % CHUNKS) * R, R)
        rows = pl.ds(start, R)
        u, q, k, kx, near = nearby(U1, p, start)
        total = src[p, rows] + near
        N[p, rows] = total
        U2[p + 1, pl.ds(start + 8, R)] = 0.2 * u + 0.8 * total / D[p, rows]
        return 0

    lax.fori_loop(0, 4 * CHUNKS, sweep_two, 0)

    def finish_two(c, _):
        start = pl.multiple_of(c * R, R)
        rows, at = pl.ds(start, R), pl.ds(start + 8, R)
        for side in range(2):
            p = 3 * side

            @pl.when(has[side])
            def _():
                arrival(2, side, c).wait_recv()
                total = N[p, rows] + 0.5 * (K[p + 1, at] + EK[side, rows]) * H[2, side, rows]
                U2[p + 1, at] = 0.2 * U1[p + 1, at] + 0.8 * total / D[p, rows]

        return 0

    lax.fori_loop(0, CHUNKS, finish_two, 0)

    present = [jnp.where(flag, 0.5, 0.0).astype(F32) for flag in has]

    def residual(c, _):
        start = pl.multiple_of(c * R, R)
        rows, at = pl.ds(start, R), pl.ds(start + 8, R)

        def row(p):
            u, q, k, kx, near = nearby(U2, p, start)
            smooth[p, rows] = u
            return src[p, rows] - D[p, rows] * u + near

        r0, r1 = row(0), row(1)
        flo = present[0] * (K[1, at] + EK[0, rows]) * U2[1, at]
        X[0, rows] = 0.625 * flo + 0.375 * r0 + 0.125 * r1
        X[1, rows] = 0.375 * flo + 0.625 * r0 + 0.875 * r1
        r2, r3 = row(2), row(3)
        fhi = present[1] * (K[4, at] + EK[1, rows]) * U2[4, at]
        X[2, rows] = 0.625 * fhi + 0.375 * r3 + 0.125 * r2
        X[1, rows] = X[1, rows] + (0.375 * fhi + 0.625 * r3 + 0.875 * r2)
        return 0

    lax.fori_loop(0, CHUNKS, residual, 0)

    def partial(side):
        return pltpu.make_async_remote_copy(
            src_ref=part.at[side],
            dst_ref=part.at[3 - side],
            send_sem=part_send.at[side],
            recv_sem=part_recv.at[1 - side],
            device_id={"brick": peer_of[side]},
            device_id_type=MESH,
        )

    def partial_in(side):
        return pltpu.make_async_remote_copy(
            src_ref=part.at[2 + side],
            dst_ref=part.at[2 + side],
            send_sem=part_send.at[side],
            recv_sem=part_recv.at[side],
            device_id={"brick": peer_of[side]},
            device_id_type=MESH,
        )

    for side in range(2):
        part[side] = to_coarse(ry[...], rz, X[2 * side])

    for side in range(2):

        @pl.when(has[side])
        def _():
            partial(side).start()

    own[...] = to_coarse(ry[...], rz, X[1])
    for side in range(2):

        @pl.when(has[side])
        def _():
            partial_in(side).wait_recv()
            own[...] = own[...] + part[2 + side]

    all_rhs[me] = own[...] * (1.0 / 64.0)

    def send_r(k, _):
        spread(all_rhs, k, r_send, r_recv).start()
        return 0

    lax.fori_loop(1, n, send_r, 0)

    def settle(k, _):
        landed(all_q, k, q_send, q_recv).wait_recv()
        landed(all_rhs, k, r_send, r_recv).wait_recv()
        spread(all_q, k, q_send, q_recv).wait_send()
        spread(all_rhs, k, r_send, r_recv).wait_send()
        return 0

    for side in range(2):

        @pl.when(has[side])
        def _():
            for c in range(CHUNKS):
                for which in range(3):
                    halo(which, side, c).wait_send()
            partial(side).wait_send()

    lax.fori_loop(1, n, settle, 0)


def coarse_kernel(
    n, group,
    owner, rhs, perm, smooth, ez, ey,
    corrected, held,
    q_pad, C, coef, B,
):
    me = lax.axis_index("brick")
    rows, lanes = rhs.shape[1:]
    cz = lanes // 2
    shape = (group, rows, lanes)
    row = lax.broadcasted_iota(jnp.int32, shape, 1)
    lane = lax.broadcasted_iota(jnp.int32, shape, 2)
    low_half = lane < cz
    z = jnp.where(low_half, lane, lane - cz)
    y_first = (row == 0) & low_half
    y_last = (row == rows - 1) & jnp.logical_not(low_half)
    z_first, z_last = z == 0, z == cz - 1

    def shifts(c):
        swapped = pltpu.roll(c, cz, 2)
        y_low = jnp.where(low_half, pltpu.roll(swapped, 1, 1), swapped)
        y_high = jnp.where(low_half, swapped, pltpu.roll(swapped, rows - 1, 1))
        return y_low, y_high, pltpu.roll(c, 1, 2), pltpu.roll(c, lanes - 1, 2)

    edge = jnp.zeros((rows, lanes), F32)
    q_pad[0] = edge
    q_pad[n + 1] = edge
    for slot in range(2):
        C[slot, 0] = edge
        C[slot, n + 1] = edge
    q_pad[1 : n + 1] = perm[...]

    def prepare(g, _):
        at = pl.multiple_of(g * group, group)
        q = q_pad[pl.ds(at + 1, group)]
        near = [q_pad[pl.ds(at, group)], q_pad[pl.ds(at + 2, group)]]
        near += [
            jnp.where(out, 0.0, v)
            for out, v in zip((y_first, y_last, z_first, z_last), shifts(q))
        ]
        faces = [0.5 * (q + v) for v in near]
        diagonal = ((faces[0] + faces[1]) + (faces[2] + faces[3])) + (faces[4] + faces[5])
        scale = 0.8 / diagonal
        for k, out in enumerate((None, None, y_first, y_last, z_first, z_last)):
            f = faces[k] * scale
            coef[k, pl.ds(at, group)] = f if out is None else jnp.where(out, 0.0, f)
        b = 16.0 * rhs[pl.ds(at, group)] * scale
        B[pl.ds(at, group)] = b
        C[0, pl.ds(at + 1, group)] = b
        return 0

    lax.fori_loop(0, n // group, prepare, 0)

    for sweep in range(SWEEPS - 1):
        now, later = sweep % 2, 1 - sweep % 2

        def step(g, _):
            at = pl.multiple_of(g * group, group)
            c = C[now, pl.ds(at + 1, group)]
            near = (C[now, pl.ds(at, group)], C[now, pl.ds(at + 2, group)]) + shifts(c)
            terms = [coef[k, pl.ds(at, group)] * v for k, v in enumerate(near)]
            total = B[pl.ds(at, group)] + 0.2 * c
            total = (total + (terms[0] + terms[1])) + ((terms[2] + terms[3]) + (terms[4] + terms[5]))
            C[later, pl.ds(at + 1, group)] = total
            return 0

        lax.fori_loop(0, n // group, step, 0)

    final = (SWEEPS - 1) % 2

    mine = jnp.zeros((rows, lanes), F32)
    for b in range(n):
        mine = jnp.where(owner[b] == me, C[final, b + 1], mine)
    for r in range(rows):
        held[0:1, r * lanes : (r + 1) * lanes] = mine[r : r + 1]

    below, mid, above = C[final, me], C[final, me + 1], C[final, me + 2]
    planes = jnp.concatenate(
        [
            0.625 * mid + 0.375 * below,
            0.875 * mid + 0.125 * below,
            0.875 * mid + 0.125 * above,
            0.625 * mid + 0.375 * above,
        ],
        axis=0,
    )
    hi, lo = split(planes)
    even = dot(hi, ez[0]) + dot(lo, ez[0])
    odd = dot(hi, ez[1]) + dot(lo, ez[1])
    for p in range(4):
        both = jnp.concatenate(
            [even[p * rows : (p + 1) * rows], odd[p * rows : (p + 1) * rows]], axis=0
        )
        hi, lo = split(both)
        corrected[p] = smooth[p] + (dot(ey[...], hi) + dot(ey[...], lo))


def local(n, source, guess, log_perm, owner):
    planes, ny, nz = source.shape
    assert planes == 4
    cells = (ny // 4) * (nz // 4)
    rows, lanes = ny // 8, nz // 2
    dense = (rows, lanes)
    as_bf16 = lambda m: jnp.asarray(m.astype(ml_dtypes.bfloat16))
    py, pz = even_odd(prolong_matrix(ny)), prolong_matrix(nz)
    ry, rz = as_bf16(py.T), as_bf16(halves(pz))
    my, mz = as_bf16(even_odd(mean_matrix(ny)).T), as_bf16(halves(mean_matrix(nz)))
    ey, ez = as_bf16(py), as_bf16(halves(pz).transpose(0, 2, 1))
    vmem = pl.BlockSpec(memory_space=pltpu.VMEM)
    anywhere = pl.BlockSpec(memory_space=pl.ANY)
    whole = lambda *s: pltpu.VMEM(s, F32)
    dma = lambda *s: pltpu.SemaphoreType.DMA(s)
    padded = (6, ny + 16, nz)
    smooth, all_rhs, all_q = pl.pallas_call(
        functools.partial(smooth_kernel, n, ny, nz),
        out_shape=(
            jax.ShapeDtypeStruct((4, ny, nz), F32),
            jax.ShapeDtypeStruct((n,) + dense, F32),
            jax.ShapeDtypeStruct((n,) + dense, F32),
        ),
        in_specs=[anywhere] * 3 + [vmem] * 4,
        out_specs=(vmem,) * 3,
        scratch_shapes=[
            whole(4, ny, nz), whole(4, ny, nz),
            whole(*padded), whole(*padded), whole(*padded), whole(*padded),
            whole(4, ny, nz), whole(4, ny, nz),
            whole(2, ny, nz), whole(3, ny, nz), whole(3, 2, ny, nz),
            whole(*dense), whole(4, *dense),
            dma(3), dma(3, 2, CHUNKS), dma(3, 2, CHUNKS), dma(2), dma(2),
            dma(n), dma(n), dma(n), dma(n),
        ],
        compiler_params=pltpu.CompilerParams(
            collective_id=0, has_side_effects=True, vmem_limit_bytes=24 * 2**20
        ),
        name="smooth",
    )(source, guess, log_perm, ry, rz, my, mz)
    return pl.pallas_call(
        functools.partial(coarse_kernel, n, min(8, n)),
        out_shape=(
            jax.ShapeDtypeStruct((4, ny, nz), F32),
            jax.ShapeDtypeStruct((1, cells), F32),
        ),
        in_specs=[pl.BlockSpec(memory_space=pltpu.SMEM)] + [vmem] * 5,
        out_specs=(vmem, vmem),
        scratch_shapes=[
            whole(n + 2, *dense), whole(2, n + 2, *dense), whole(6, n, *dense), whole(n, *dense),
        ],
        compiler_params=pltpu.CompilerParams(vmem_limit_bytes=24 * 2**20),
        name="coarse",
    )(owner, all_rhs, all_q, smooth, ez, ey)


def solution(mesh):
    spec = P(("samples", "brick"), None, None)
    return jax.shard_map(
        functools.partial(local, mesh.shape["brick"]),
        mesh=mesh,
        in_specs=(spec, spec, spec, P()),
        out_specs=(spec, P(("samples", "brick"), None)),
        check_vma=False,
    )
```

time: 213 us -> 38.4 us (0.18)
  waiting for transfers between devices: 88.9 us -> 0 us
  blocking collectives: 46.4 us -> 0 us
  Pallas kernels: 0 us -> 30.4 us
  starting transfers between devices: 20.6 us -> 0 us
  between operations: 18.7 us -> 0.68 us
  other arithmetic: 15.6 us -> 0 us
  local copies, waits for them, and re-layouts: 16.8 us -> 6.95 us
  matrix products: 5.18 us -> 0 us
    unnamed x2 -> x0, waiting for transfers between devices: 87.5 us -> none
    all_gather x2 -> x0, blocking collectives: 46.4 us -> none  [the longest x1 23.8 us: local(): lax.all_gather(coarse_own, 'brick', axis=0, tiled=True)]
    pallas_call x0 -> x2, Pallas kernels: none -> 30.4 us  [the longest x1 26.6 us: local(): pl.pallas_call(functools.partial(smooth_kernel, n, ny, nz), out_shape=(ja...]
    ppermute x8 -> x0, starting transfers between devices: 20.5 us -> none  [the longest x4 15.4 us: with_halo(): lax.ppermute(lax.slice_in_dim(block, block.shape[dim] - width, None, axis...]
    add x11 -> x0, other arithmetic: 7.33 us -> none  [the longest x2 4.4 us: local(): smooth = smooth + relax_weight * (source - image) / diagonal]
    reduce_sum x1 -> x0, local copies, waits for them, and re-layouts: 5.67 us -> none  [local(): perm.reshape(cpd, 4, cyc, 4, czc, 4).sum(axis=(1, 3, 5)) * (1.0 / 64.0)]
    dot_general x6 -> x0, matrix products: 5.18 us -> none  [the longest x1 2.38 us: local(): step_one = jnp.einsum('xyz,yY->xYz', resid, py, precision=hp)]
    slice x30 -> x0, local copies, waits for them, and re-layouts: 4.74 us -> none  [the longest x2 1.51 us: cols_up(): return jnp.pad(a[:, width:], ((0, 0), (0, width)))]
  transfers between devices with their start and end apart: 9 -> 0, of which waited for: 2 -> 0; matrix products, arithmetic and copies ran while one was open for 7% -> 0% of each run, Pallas kernels for 0% -> 0%
where the time goes in v1:
time: 38.4 us; the launch traced here: 38 us
  Pallas kernels  30.4 us (79%)
  local copies, waits for them, and re-layouts  6.95 us (18%)
  between operations  0.68 us (2%)
    pallas_call x1, Pallas kernels, local(): pl.pallas_call(functools.partial(smooth_kernel, n, ny, nz), out_shape=(ja...  26.6 us
    unnamed x20, local copies, waits for them, and re-layouts  6.95 us
    pallas_call x1, Pallas kernels, local(): pl.pallas_call(functools.partial(coarse_kernel, n, min(8, n)), out_shape=...  3.81 us

profile of v1, /device:TPU:0, one launch (start us, length us, event | category | flops | bytes accessed | tf_op | source)
XLA Modules:
  0.0 38.0 jit_solution(11696803985277302490)
XLA Ops:
  0.6 0.0 copy-start
  0.6 1.0 %copy-done = f32[4,128,256]{2,1,0:T(8,128)S(1)} copy-done((f32[4,128,256]{2,1,0:T(8,128)S(1)}, f32[4,128,256]{2,1,0:T(8,128)}, u32[]{:S(2)}) %copy-start) | copy-done | bytes 524312
  1.7 0.0 copy-start.1
  1.7 1.0 %copy-done.1 = f32[4,128,256]{2,1,0:T(8,128)S(1)} copy-done((f32[4,128,256]{2,1,0:T(8,128)S(1)}, f32[4,128,256]{2,1,0:T(8,128)}, u32[]{:S(2)}) %copy-start.1) | copy-done | bytes 524312
  2.7 0.0 copy-start.2
  2.7 1.0 %copy-done.2 = f32[4,128,256]{2,1,0:T(8,128)S(1)} copy-done((f32[4,128,256]{2,1,0:T(8,128)S(1)}, f32[4,128,256]{2,1,0:T(8,128)}, u32[]{:S(2)}) %copy-start.2) | copy-done | bytes 524312
  3.8 0.0 copy-start.3
  3.8 0.9 %copy-done.3 = bf16[2,256,128]{2,1,0:T(8,128)(2,1)S(1)} copy-done((bf16[2,256,128]{2,1,0:T(8,128)(2,1)S(1)}, bf16[2,256,128]{2,1,0:T(8,128)(2,1)}, u32[]{:S(2)}) %copy-start.3) | copy-done | bytes 131096
  4.7 0.0 copy-start.4
  4.7 0.9 %copy-done.4 = bf16[2,256,128]{2,1,0:T(8,128)(2,1)S(1)} copy-done((bf16[2,256,128]{2,1,0:T(8,128)(2,1)S(1)}, bf16[2,256,128]{2,1,0:T(8,128)(2,1)}, u32[]{:S(2)}) %copy-start.4) | copy-done | bytes 131096
  5.6 0.0 copy-start.7
  5.6 0.7 %copy-done.7 = bf16[32,128]{1,0:T(8,128)(2,1)S(1)} copy-done((bf16[32,128]{1,0:T(8,128)(2,1)S(1)}, bf16[32,128]{1,0:T(8,128)(2,1)}, u32[]{:S(2)}) %copy-start.7) | copy-done | bytes 8216
  6.3 0.0 copy-start.8
  6.3 0.7 %copy-done.8 = bf16[32,128]{1,0:T(8,128)(2,1)S(1)} copy-done((bf16[32,128]{1,0:T(8,128)(2,1)S(1)}, bf16[32,128]{1,0:T(8,128)(2,1)}, u32[]{:S(2)}) %copy-start.8) | copy-done | bytes 8216
  7.0 0.0 copy-start.5
  7.0 0.0 copy-start.6
  7.0 26.6 %smooth.1 = (f32[4,128,256]{2,1,0:T(8,128)S(1)}, f32[16,16,128]{2,1,0:T(8,128)S(1)}, f32[16,16,128]{2,1,0:T(8,128)S(1)}) custom-call(f32[4,128,256]{2,1,0:T(8,128)S(1)} %copy-done, f32[4,128,256]{2,1,0:T(8,128)S(1)} %copy-done.1, f32[4,128,256]{2,1,0:T(8,128)S(1)} %copy-done.2, bf16[32,128]{1,0:T(8,128)(2,1)S(1)} %copy-done.8, ...), custom_call_target="tpu_custom_call" | custom-call | tf_op jit(solution)/shard_map/smooth/pallas_call | solution.py:471
  33.6 0.0 copy-start.9
  33.6 0.0 copy-done.5
  33.6 0.0 copy-done.6
  33.6 0.6 %copy-done.9 = s32[16]{0:T(128)S(1)} copy-done((s32[16]{0:T(128)S(1)}, s32[16]{0:T(128)}, u32[]{:S(2)}) %copy-start.9) | copy-done | bytes 88
  34.2 3.8 %coarse.1 = (f32[4,128,256]{2,1,0:T(8,128)}, f32[1,2048]{1,0:T(1,128)}) custom-call(s32[16]{0:T(128)S(1)} %copy-done.9, f32[16,16,128]{2,1,0:T(8,128)S(1)} %get-tuple-element.5.rhs, f32[16,16,128]{2,1,0:T(8,128)S(1)} %get-tuple-element.6.perm, f32[4,128,256]{2,1,0:T(8,128)S(1)} %get-tuple-element.7.smooth, bf16[2,128,256]{2,1,0:T(8,128)(2,1)S(1)} %copy-done.5, ...), custom_call_target="tpu_custom_call" | custom-call | tf_op jit(solution)/shard_map/coarse/pallas_call | solution.py:494
Async XLA Ops:
  0.6 1.0 %copy-start = (f32[4,128,256]{2,1,0:T(8,128)S(1)}, f32[4,128,256]{2,1,0:T(8,128)}, u32[]{:S(2)}) copy-start(f32[4,128,256]{2,1,0:T(8,128)} %source_hbm.1) | copy-start | bytes 1572868
  1.7 1.0 %copy-start.1 = (f32[4,128,256]{2,1,0:T(8,128)S(1)}, f32[4,128,256]{2,1,0:T(8,128)}, u32[]{:S(2)}) copy-start(f32[4,128,256]{2,1,0:T(8,128)} %guess_hbm.1) | copy-start | bytes 1572868
  2.7 1.0 %copy-start.2 = (f32[4,128,256]{2,1,0:T(8,128)S(1)}, f32[4,128,256]{2,1,0:T(8,128)}, u32[]{:S(2)}) copy-start(f32[4,128,256]{2,1,0:T(8,128)} %logq_hbm.1) | copy-start | bytes 1572868
  3.8 0.9 %copy-start.3 = (bf16[2,256,128]{2,1,0:T(8,128)(2,1)S(1)}, bf16[2,256,128]{2,1,0:T(8,128)(2,1)}, u32[]{:S(2)}) copy-start(bf16[2,256,128]{2,1,0:T(8,128)(2,1)} %constant.15.clone.mz) | copy-start | bytes 393220
  4.7 0.9 %copy-start.4 = (bf16[2,256,128]{2,1,0:T(8,128)(2,1)S(1)}, bf16[2,256,128]{2,1,0:T(8,128)(2,1)}, u32[]{:S(2)}) copy-start(bf16[2,256,128]{2,1,0:T(8,128)(2,1)} %constant.13.clone.rz) | copy-start | bytes 393220
  5.6 0.7 %copy-start.7 = (bf16[32,128]{1,0:T(8,128)(2,1)S(1)}, bf16[32,128]{1,0:T(8,128)(2,1)}, u32[]{:S(2)}) copy-start(bf16[32,128]{1,0:T(8,128)(2,1)} %constant.14.clone.my) | copy-start | bytes 24580
  6.3 0.7 %copy-start.8 = (bf16[32,128]{1,0:T(8,128)(2,1)S(1)}, bf16[32,128]{1,0:T(8,128)(2,1)}, u32[]{:S(2)}) copy-start(bf16[32,128]{1,0:T(8,128)(2,1)} %constant.12.clone.ry) | copy-start | bytes 24580
  7.0 26.6 %copy-start.5 = (bf16[2,128,256]{2,1,0:T(8,128)(2,1)S(1)}, bf16[2,128,256]{2,1,0:T(8,128)(2,1)}, u32[]{:S(2)}) copy-start(bf16[2,128,256]{2,1,0:T(8,128)(2,1)} %constant.17.clone.ez) | copy-start | bytes 393220
  7.0 26.6 %copy-start.6 = (bf16[128,32]{1,0:T(8,128)(2,1)S(1)}, bf16[128,32]{1,0:T(8,128)(2,1)}, u32[]{:S(2)}) copy-start(bf16[128,32]{1,0:T(8,128)(2,1)} %constant.16.clone.ey) | copy-start | bytes 24580
  33.6 0.7 %copy-start.9 = (s32[16]{0:T(128)S(1)}, s32[16]{0:T(128)}, u32[]{:S(2)}) copy-start(s32[16]{0:T(128)} %owner.1) | copy-start | bytes 196

commit v2 on v1

--- a/solution.py
+++ b/solution.py
@@ -61,9 +61,9 @@
 
 def smooth_kernel(
     n, ny, nz,
-    source_hbm, guess_hbm, logq_hbm, ry, rz, my, mz,
-    smooth, all_rhs, all_q,
-    src, logq, K, U0, U1, U2, D, N, EK, X, H, own, part,
+    source_hbm, guess_hbm, logq_hbm, ry_hbm, rz_hbm, my_hbm, mz_hbm,
+    smooth_hbm, all_rhs, coef_hbm, scaled_hbm,
+    coef, scaled, ry, rz, my, mz, all_q, q_pad, src, logq, K, U0, U1, U2, D, N, EK, X, H, own, part,
     local_sem, halo_send, halo_recv, part_send, part_recv, q_send, q_recv, r_send, r_recv,
 ):
     me = lax.axis_index("brick")
@@ -75,6 +75,10 @@
         pltpu.make_async_copy(logq_hbm, logq, local_sem.at[0]),
         pltpu.make_async_copy(guess_hbm, U0.at[pl.ds(1, 4), pl.ds(8, ny)], local_sem.at[1]),
         pltpu.make_async_copy(source_hbm, src, local_sem.at[2]),
+        pltpu.make_async_copy(my_hbm, my, local_sem.at[3]),
+        pltpu.make_async_copy(mz_hbm, mz, local_sem.at[4]),
+        pltpu.make_async_copy(ry_hbm, ry, local_sem.at[5]),
+        pltpu.make_async_copy(rz_hbm, rz, local_sem.at[6]),
     ]
     for copy in loads:
         copy.start()
@@ -153,8 +157,8 @@
         return 0
 
     lax.fori_loop(0, 4 * CHUNKS, exps, 0)
-    loads[1].wait()
-    loads[2].wait()
+    for copy in loads[1:]:
+        copy.wait()
 
     def nearby(U, p, start):
         at = pl.ds(start + 8, R)
@@ -212,11 +216,9 @@
 
         return 0
 
-    lax.fori_loop(0, CHUNKS, finish_one, 0)
-
-    def spread(ref, k, send, recv):
+    def spread(block, ref, k, send, recv):
         return pltpu.make_async_remote_copy(
-            src_ref=ref.at[me],
+            src_ref=block,
             dst_ref=ref.at[me],
             send_sem=send.at[k],
             recv_sem=recv.at[me],
@@ -236,13 +238,10 @@
         )
 
     def send_q(k, _):
-        spread(all_q, k, q_send, q_recv).start()
-        return 0
-
-    lax.fori_loop(1, n, send_q, 0)
-
-    def sweep_two(i, _):
-        p, start = i // CHUNKS, pl.multiple_of((i % CHUNKS) * R, R)
+        spread(all_q.at[me], all_q, k, q_send, q_recv).start()
+        return 0
+
+    def sweep_two(p, start):
         rows = pl.ds(start, R)
         u, q, k, kx, near = nearby(U1, p, start)
         total = src[p, rows] + near
@@ -250,7 +249,23 @@
         U2[p + 1, pl.ds(start + 8, R)] = 0.2 * u + 0.8 * total / D[p, rows]
         return 0
 
-    lax.fori_loop(0, 4 * CHUNKS, sweep_two, 0)
+    def first_stage(c, _):
+        @pl.when(c < CHUNKS)
+        def _():
+            finish_one(c, 0)
+
+        @pl.when(c == CHUNKS - 1)
+        def _():
+            lax.fori_loop(1, n, send_q, 0)
+
+        @pl.when(c > 0)
+        def _():
+            start = pl.multiple_of((c - 1) * R, R)
+            lax.fori_loop(0, 4, lambda p, _: sweep_two(p, start), 0)
+
+        return 0
+
+    lax.fori_loop(0, CHUNKS + 1, first_stage, 0)
 
     def finish_two(c, _):
         start = pl.multiple_of(c * R, R)
@@ -266,8 +281,6 @@
 
         return 0
 
-    lax.fori_loop(0, CHUNKS, finish_two, 0)
-
     present = [jnp.where(flag, 0.5, 0.0).astype(F32) for flag in has]
 
     def residual(c, _):
@@ -276,7 +289,6 @@
 
         def row(p):
             u, q, k, kx, near = nearby(U2, p, start)
-            smooth[p, rows] = u
             return src[p, rows] - D[p, rows] * u + near
 
         r0, r1 = row(0), row(1)
@@ -289,7 +301,26 @@
         X[1, rows] = X[1, rows] + (0.375 * fhi + 0.625 * r3 + 0.875 * r2)
         return 0
 
-    lax.fori_loop(0, CHUNKS, residual, 0)
+    def second_stage(c, _):
+        @pl.when(c < CHUNKS)
+        def _():
+            finish_two(c, 0)
+
+        @pl.when(c > 0)
+        def _():
+            residual(c - 1, 0)
+
+        return 0
+
+    lax.fori_loop(0, CHUNKS + 1, second_stage, 0)
+
+    stores = [
+        pltpu.make_async_copy(U2.at[pl.ds(1, 4), pl.ds(8, ny)], smooth_hbm, local_sem.at[0]),
+        pltpu.make_async_copy(own, all_rhs.at[me], local_sem.at[1]),
+        pltpu.make_async_copy(coef, coef_hbm, local_sem.at[2]),
+        pltpu.make_async_copy(scaled, scaled_hbm, local_sem.at[3]),
+    ]
+    stores[0].start()
 
     def partial(side):
         return pltpu.make_async_remote_copy(
@@ -328,20 +359,29 @@
             partial_in(side).wait_recv()
             own[...] = own[...] + part[2 + side]
 
-    all_rhs[me] = own[...] * (1.0 / 64.0)
+    own[...] = own[...] * (1.0 / 64.0)
+    stores[1].start()
 
     def send_r(k, _):
-        spread(all_rhs, k, r_send, r_recv).start()
+        spread(own, all_rhs, k, r_send, r_recv).start()
         return 0
 
     lax.fori_loop(1, n, send_r, 0)
 
-    def settle(k, _):
+    def settle_q(k, _):
         landed(all_q, k, q_send, q_recv).wait_recv()
+        spread(all_q.at[me], all_q, k, q_send, q_recv).wait_send()
+        return 0
+
+    def settle_r(k, _):
         landed(all_rhs, k, r_send, r_recv).wait_recv()
-        spread(all_q, k, q_send, q_recv).wait_send()
-        spread(all_rhs, k, r_send, r_recv).wait_send()
-        return 0
+        spread(own, all_rhs, k, r_send, r_recv).wait_send()
+        return 0
+
+    lax.fori_loop(1, n, settle_q, 0)
+    coarse_coefficients(n, min(8, n), all_q, q_pad, coef, scaled)
+    stores[2].start()
+    stores[3].start()
 
     for side in range(2):
 
@@ -352,26 +392,24 @@
                     halo(which, side, c).wait_send()
             partial(side).wait_send()
 
-    lax.fori_loop(1, n, settle, 0)
-
-
-def coarse_kernel(
-    n, group,
-    owner, rhs, perm, smooth, ez, ey,
-    corrected, held,
-    q_pad, C, coef, B,
-):
-    me = lax.axis_index("brick")
-    rows, lanes = rhs.shape[1:]
+    lax.fori_loop(1, n, settle_r, 0)
+    for copy in stores:
+        copy.wait()
+
+
+def coarse_shifts(shape):
+    rows, lanes = shape[1:]
     cz = lanes // 2
-    shape = (group, rows, lanes)
     row = lax.broadcasted_iota(jnp.int32, shape, 1)
     lane = lax.broadcasted_iota(jnp.int32, shape, 2)
     low_half = lane < cz
     z = jnp.where(low_half, lane, lane - cz)
-    y_first = (row == 0) & low_half
-    y_last = (row == rows - 1) & jnp.logical_not(low_half)
-    z_first, z_last = z == 0, z == cz - 1
+    outside = (
+        (row == 0) & low_half,
+        (row == rows - 1) & jnp.logical_not(low_half),
+        z == 0,
+        z == cz - 1,
+    )
 
     def shifts(c):
         swapped = pltpu.roll(c, cz, 2)
@@ -379,35 +417,64 @@
         y_high = jnp.where(low_half, swapped, pltpu.roll(swapped, rows - 1, 1))
         return y_low, y_high, pltpu.roll(c, 1, 2), pltpu.roll(c, lanes - 1, 2)
 
+    return shifts, outside
+
+
+def coarse_coefficients(n, group, perm, q_pad, coef, scaled):
+    rows, lanes = perm.shape[1:]
+    shifts, outside = coarse_shifts((group, rows, lanes))
     edge = jnp.zeros((rows, lanes), F32)
     q_pad[0] = edge
     q_pad[n + 1] = edge
-    for slot in range(2):
-        C[slot, 0] = edge
-        C[slot, n + 1] = edge
     q_pad[1 : n + 1] = perm[...]
 
     def prepare(g, _):
         at = pl.multiple_of(g * group, group)
         q = q_pad[pl.ds(at + 1, group)]
         near = [q_pad[pl.ds(at, group)], q_pad[pl.ds(at + 2, group)]]
-        near += [
-            jnp.where(out, 0.0, v)
-            for out, v in zip((y_first, y_last, z_first, z_last), shifts(q))
-        ]
+        near += [jnp.where(out, 0.0, v) for out, v in zip(outside, shifts(q))]
         faces = [0.5 * (q + v) for v in near]
         diagonal = ((faces[0] + faces[1]) + (faces[2] + faces[3])) + (faces[4] + faces[5])
         scale = 0.8 / diagonal
-        for k, out in enumerate((None, None, y_first, y_last, z_first, z_last)):
+        for k, out in enumerate((None, None) + outside):
             f = faces[k] * scale
             coef[k, pl.ds(at, group)] = f if out is None else jnp.where(out, 0.0, f)
-        b = 16.0 * rhs[pl.ds(at, group)] * scale
-        B[pl.ds(at, group)] = b
-        C[0, pl.ds(at + 1, group)] = b
+        scaled[pl.ds(at, group)] = 16.0 * scale
         return 0
 
     lax.fori_loop(0, n // group, prepare, 0)
 
+
+def coarse_kernel(
+    n, group,
+    owner_hbm, rhs_hbm, coef_hbm, scaled_hbm, smooth_hbm, ez_hbm, ey_hbm,
+    corrected_hbm, held,
+    owner, rhs, coef, scaled, smooth, ez, ey, C, B, corrected, sem,
+):
+    me = lax.axis_index("brick")
+    loads = [
+        pltpu.make_async_copy(*pair, sem.at[4 + k])
+        for k, pair in enumerate(
+            (
+                (rhs_hbm, rhs), (scaled_hbm, scaled), (coef_hbm, coef),
+                (ez_hbm, ez), (ey_hbm, ey), (smooth_hbm, smooth), (owner_hbm, owner),
+            )
+        )
+    ]
+    for load in loads:
+        load.start()
+    rows, lanes = rhs.shape[1:]
+    shifts, _ = coarse_shifts((group, rows, lanes))
+    edge = jnp.zeros((rows, lanes), F32)
+    for slot in range(2):
+        C[slot, 0] = edge
+        C[slot, n + 1] = edge
+    loads[0].wait()
+    loads[1].wait()
+    B[...] = rhs[...] * scaled[...]
+    C[0, 1 : n + 1] = B[...]
+
+    loads[2].wait()
     for sweep in range(SWEEPS - 1):
         now, later = sweep % 2, 1 - sweep % 2
 
@@ -425,12 +492,8 @@
 
     final = (SWEEPS - 1) % 2
 
-    mine = jnp.zeros((rows, lanes), F32)
-    for b in range(n):
-        mine = jnp.where(owner[b] == me, C[final, b + 1], mine)
-    for r in range(rows):
-        held[0:1, r * lanes : (r + 1) * lanes] = mine[r : r + 1]
-
+    for load in loads[3:]:
+        load.wait()
     below, mid, above = C[final, me], C[final, me + 1], C[final, me + 2]
     planes = jnp.concatenate(
         [
@@ -450,6 +513,15 @@
         )
         hi, lo = split(both)
         corrected[p] = smooth[p] + (dot(ey[...], hi) + dot(ey[...], lo))
+        pltpu.make_async_copy(corrected.at[p], corrected_hbm.at[p], sem.at[p]).start()
+
+    mine = jnp.zeros((rows, lanes), F32)
+    for b in range(n):
+        mine = jnp.where(owner[b] == me, C[final, b + 1], mine)
+    for r in range(rows):
+        held[0:1, r * lanes : (r + 1) * lanes] = mine[r : r + 1]
+    for p in range(4):
+        pltpu.make_async_copy(corrected.at[p], corrected_hbm.at[p], sem.at[p]).wait()
 
 
 def local(n, source, guess, log_perm, owner):
@@ -464,30 +536,35 @@
     my, mz = as_bf16(even_odd(mean_matrix(ny)).T), as_bf16(halves(mean_matrix(nz)))
     ey, ez = as_bf16(py), as_bf16(halves(pz).transpose(0, 2, 1))
     vmem = pl.BlockSpec(memory_space=pltpu.VMEM)
-    anywhere = pl.BlockSpec(memory_space=pl.ANY)
+    hbm = pl.BlockSpec(memory_space=pl.ANY)
     whole = lambda *s: pltpu.VMEM(s, F32)
     dma = lambda *s: pltpu.SemaphoreType.DMA(s)
     padded = (6, ny + 16, nz)
-    smooth, all_rhs, all_q = pl.pallas_call(
+    smooth, all_rhs, coef, scaled = pl.pallas_call(
         functools.partial(smooth_kernel, n, ny, nz),
         out_shape=(
             jax.ShapeDtypeStruct((4, ny, nz), F32),
             jax.ShapeDtypeStruct((n,) + dense, F32),
+            jax.ShapeDtypeStruct((6, n) + dense, F32),
             jax.ShapeDtypeStruct((n,) + dense, F32),
         ),
-        in_specs=[anywhere] * 3 + [vmem] * 4,
-        out_specs=(vmem,) * 3,
+        in_specs=[hbm] * 7,
+        out_specs=(hbm,) * 4,
         scratch_shapes=[
+            whole(6, n, *dense), whole(n, *dense),
+            pltpu.VMEM(ry.shape, BF16), pltpu.VMEM(rz.shape, BF16),
+            pltpu.VMEM(my.shape, BF16), pltpu.VMEM(mz.shape, BF16),
+            whole(n, *dense), whole(n + 2, *dense),
             whole(4, ny, nz), whole(4, ny, nz),
             whole(*padded), whole(*padded), whole(*padded), whole(*padded),
             whole(4, ny, nz), whole(4, ny, nz),
             whole(2, ny, nz), whole(3, ny, nz), whole(3, 2, ny, nz),
             whole(*dense), whole(4, *dense),
-            dma(3), dma(3, 2, CHUNKS), dma(3, 2, CHUNKS), dma(2), dma(2),
+            dma(7), dma(3, 2, CHUNKS), dma(3, 2, CHUNKS), dma(2), dma(2),
             dma(n), dma(n), dma(n), dma(n),
         ],
         compiler_params=pltpu.CompilerParams(
-            collective_id=0, has_side_effects=True, vmem_limit_bytes=24 * 2**20
+            collective_id=0, has_side_effects=True, vmem_limit_bytes=60 * 2**20
         ),
         name="smooth",
     )(source, guess, log_perm, ry, rz, my, mz)
@@ -497,14 +574,17 @@
             jax.ShapeDtypeStruct((4, ny, nz), F32),
             jax.ShapeDtypeStruct((1, cells), F32),
         ),
-        in_specs=[pl.BlockSpec(memory_space=pltpu.SMEM)] + [vmem] * 5,
-        out_specs=(vmem, vmem),
+        in_specs=[hbm] * 7,
+        out_specs=(hbm, vmem),
         scratch_shapes=[
-            whole(n + 2, *dense), whole(2, n + 2, *dense), whole(6, n, *dense), whole(n, *dense),
+            pltpu.SMEM((n,), jnp.int32),
+            whole(n, *dense), whole(6, n, *dense), whole(n, *dense), whole(4, ny, nz),
+            pltpu.VMEM(ez.shape, BF16), pltpu.VMEM(ey.shape, BF16),
+            whole(2, n + 2, *dense), whole(n, *dense), whole(4, ny, nz), dma(11),
         ],
-        compiler_params=pltpu.CompilerParams(vmem_limit_bytes=24 * 2**20),
+        compiler_params=pltpu.CompilerParams(vmem_limit_bytes=60 * 2**20),
         name="coarse",
-    )(owner, all_rhs, all_q, smooth, ez, ey)
+    )(owner, all_rhs, coef, scaled, smooth, ez, ey)
 
 
 def solution(mesh):

time: 38.4 us -> 32 us (0.83)
  local copies, waits for them, and re-layouts: 6.95 us -> 0 us
  Pallas kernels: 30.4 us -> 31.2 us
    unnamed x20 -> x0, local copies, waits for them, and re-layouts: 6.95 us -> none
    pallas_call x1, Pallas kernels: 3.81 us -> 4.84 us  [local(): pl.pallas_call(functools.partial(coarse_kernel, n, min(8, n)), out_shape=...]
where the time goes in v2:
time: 32 us; the launch traced here: 31.8 us
  Pallas kernels  31.2 us (98%)
  between operations  0.64 us (2%)
    pallas_call x1, Pallas kernels, local(): pl.pallas_call(functools.partial(smooth_kernel, n, ny, nz), out_shape=(ja...  26.4 us
    pallas_call x1, Pallas kernels, local(): pl.pallas_call(functools.partial(coarse_kernel, n, min(8, n)), out_shape=...  4.84 us

profile of v2, /device:TPU:0, one launch (start us, length us, event | category | flops | bytes accessed | tf_op | source)
XLA Modules:
  0.0 31.8 jit_solution(13516582051546738972)
XLA Ops:
  0.6 26.4 %smooth.1 = (f32[4,128,256]{2,1,0:T(8,128)}, f32[16,16,128]{2,1,0:T(8,128)}, f32[6,16,16,128]{3,2,1,0:T(8,128)}, f32[16,16,128]{2,1,0:T(8,128)}) custom-call(f32[4,128,256]{2,1,0:T(8,128)} %source_hbm.1, f32[4,128,256]{2,1,0:T(8,128)} %guess_hbm.1, f32[4,128,256]{2,1,0:T(8,128)} %logq_hbm.1, bf16[32,128]{1,0:T(8,128)(2,1)} %constant.12.clone.ry_hbm, ...), custom_call_target="tpu_custom_call" | custom-call | tf_op jit(solution)/shard_map/smooth/pallas_call | solution.py:543
  27.0 4.8 %coarse.1 = (f32[4,128,256]{2,1,0:T(8,128)}, f32[1,2048]{1,0:T(1,128)}) custom-call(s32[16]{0:T(128)} %owner_hbm.1, f32[16,16,128]{2,1,0:T(8,128)} %get-tuple-element.6.rhs_hbm, f32[6,16,16,128]{3,2,1,0:T(8,128)} %get-tuple-element.7.coef_hbm, f32[16,16,128]{2,1,0:T(8,128)} %get-tuple-element.8.scaled_hbm, f32[4,128,256]{2,1,0:T(8,128)} %get-tuple-element.9.smooth_hbm, ...), custom_call_target="tpu_custom_call" | custom-call | tf_op jit(solution)/shard_map/coarse/pallas_call | solution.py:571

commit v3 on v2

--- a/solution.py
+++ b/solution.py
@@ -10,7 +10,7 @@
 from jax.sharding import PartitionSpec as P
 
 SWEEPS = 8
-CHUNKS = 4
+CHUNKS = 8
 MESH = pl.DeviceIdType.MESH
 F32 = jnp.float32
 BF16 = jnp.bfloat16

time: 32 us -> 31.1 us (0.972)
  Pallas kernels: 31.2 us -> 30.3 us
    pallas_call x1, Pallas kernels: 26.4 us -> 25.5 us  [local(): pl.pallas_call(functools.partial(smooth_kernel, n, ny, nz), out_shape=(ja...]
where the time goes in v3:
time: 31.1 us; the launch traced here: 31 us
  Pallas kernels  30.3 us (97%)
  between operations  0.64 us (2%)
    pallas_call x1, Pallas kernels, local(): pl.pallas_call(functools.partial(smooth_kernel, n, ny, nz), out_shape=(ja...  25.5 us
    pallas_call x1, Pallas kernels, local(): pl.pallas_call(functools.partial(coarse_kernel, n, min(8, n)), out_shape=...  4.84 us

profile of v3, /device:TPU:0, one launch (start us, length us, event | category | flops | bytes accessed | tf_op | source)
XLA Modules:
  0.0 31.0 jit_solution(12965486069834616069)
XLA Ops:
  0.6 25.5 %smooth.1 = (f32[4,128,256]{2,1,0:T(8,128)}, f32[16,16,128]{2,1,0:T(8,128)}, f32[6,16,16,128]{3,2,1,0:T(8,128)}, f32[16,16,128]{2,1,0:T(8,128)}) custom-call(f32[4,128,256]{2,1,0:T(8,128)} %source_hbm.1, f32[4,128,256]{2,1,0:T(8,128)} %guess_hbm.1, f32[4,128,256]{2,1,0:T(8,128)} %logq_hbm.1, bf16[32,128]{1,0:T(8,128)(2,1)} %constant.12.clone.ry_hbm, ...), custom_call_target="tpu_custom_call" | custom-call | tf_op jit(solution)/shard_map/smooth/pallas_call | solution.py:543
  26.1 4.8 %coarse.1 = (f32[4,128,256]{2,1,0:T(8,128)}, f32[1,2048]{1,0:T(1,128)}) custom-call(s32[16]{0:T(128)} %owner_hbm.1, f32[16,16,128]{2,1,0:T(8,128)} %get-tuple-element.6.rhs_hbm, f32[6,16,16,128]{3,2,1,0:T(8,128)} %get-tuple-element.7.coef_hbm, f32[16,16,128]{2,1,0:T(8,128)} %get-tuple-element.8.scaled_hbm, f32[4,128,256]{2,1,0:T(8,128)} %get-tuple-element.9.smooth_hbm, ...), custom_call_target="tpu_custom_call" | custom-call | tf_op jit(solution)/shard_map/coarse/pallas_call | solution.py:571

commit v4 on v3

--- a/solution.py
+++ b/solution.py
@@ -569,7 +569,7 @@
         name="smooth",
     )(source, guess, log_perm, ry, rz, my, mz)
     return pl.pallas_call(
-        functools.partial(coarse_kernel, n, min(8, n)),
+        functools.partial(coarse_kernel, n, min(16, n)),
         out_shape=(
             jax.ShapeDtypeStruct((4, ny, nz), F32),
             jax.ShapeDtypeStruct((1, cells), F32),

time: 31.1 us -> 30.5 us (0.981)
  Pallas kernels: 30.3 us -> 29.7 us
    pallas_call x1, Pallas kernels: 4.84 us -> 4.18 us  [local(): pl.pallas_call(functools.partial(coarse_kernel, n, min(16, n)), out_shape...]
where the time goes in v4:
time: 30.5 us; the launch traced here: 30.3 us
  Pallas kernels  29.7 us (97%)
  between operations  0.64 us (2%)
    pallas_call x1, Pallas kernels, local(): pl.pallas_call(functools.partial(smooth_kernel, n, ny, nz), out_shape=(ja...  25.5 us
    pallas_call x1, Pallas kernels, local(): pl.pallas_call(functools.partial(coarse_kernel, n, min(16, n)), out_shape...  4.18 us

profile of v4, /device:TPU:0, one launch (start us, length us, event | category | flops | bytes accessed | tf_op | source)
XLA Modules:
  0.0 30.3 jit_solution(9451257044342322843)
XLA Ops:
  0.6 25.5 %smooth.1 = (f32[4,128,256]{2,1,0:T(8,128)}, f32[16,16,128]{2,1,0:T(8,128)}, f32[6,16,16,128]{3,2,1,0:T(8,128)}, f32[16,16,128]{2,1,0:T(8,128)}) custom-call(f32[4,128,256]{2,1,0:T(8,128)} %source_hbm.1, f32[4,128,256]{2,1,0:T(8,128)} %guess_hbm.1, f32[4,128,256]{2,1,0:T(8,128)} %logq_hbm.1, bf16[32,128]{1,0:T(8,128)(2,1)} %constant.12.clone.ry_hbm, ...), custom_call_target="tpu_custom_call" | custom-call | tf_op jit(solution)/shard_map/smooth/pallas_call | solution.py:543
  26.1 4.2 %coarse.1 = (f32[4,128,256]{2,1,0:T(8,128)}, f32[1,2048]{1,0:T(1,128)}) custom-call(s32[16]{0:T(128)} %owner_hbm.1, f32[16,16,128]{2,1,0:T(8,128)} %get-tuple-element.6.rhs_hbm, f32[6,16,16,128]{3,2,1,0:T(8,128)} %get-tuple-element.7.coef_hbm, f32[16,16,128]{2,1,0:T(8,128)} %get-tuple-element.8.scaled_hbm, f32[4,128,256]{2,1,0:T(8,128)} %get-tuple-element.9.smooth_hbm, ...), custom_call_target="tpu_custom_call" | custom-call | tf_op jit(solution)/shard_map/coarse/pallas_call | solution.py:571

commit v5 on v4

--- a/solution.py
+++ b/solution.py
@@ -140,14 +140,13 @@
             ref[p, 0:8] = zero_rows
             ref[p, ny + 8 : ny + 16] = zero_rows
 
-    lane = lax.broadcasted_iota(jnp.int32, (R, nz), 1)
-    first, last = lane == 0, lane == nz - 1
-
     def yz(window):
-        center = window[8 : R + 8]
-        low = jnp.where(first, 0.0, pltpu.roll(center, 1, 1))
-        high = jnp.where(last, 0.0, pltpu.roll(center, nz - 1, 1))
-        return (window[7 : R + 7] + window[9 : R + 9]) + (low + high)
+        size = window.shape[0] - 16
+        lane = lax.broadcasted_iota(jnp.int32, (size, nz), 1)
+        center = window[8 : size + 8]
+        low = jnp.where(lane == 0, 0.0, pltpu.roll(center, 1, 1))
+        high = jnp.where(lane == nz - 1, 0.0, pltpu.roll(center, nz - 1, 1))
+        return (window[7 : size + 7] + window[9 : size + 9]) + (low + high)
 
     loads[0].wait()
 
@@ -160,28 +159,28 @@
     for copy in loads[1:]:
         copy.wait()
 
-    def nearby(U, p, start):
-        at = pl.ds(start + 8, R)
-        window = pl.ds(start, R + 16)
+    def nearby(U, p, start, size=R):
+        at = pl.ds(start + 8, size)
+        window = pl.ds(start, size + 16)
         u, k = U[p + 1, window], K[p + 1, window]
         um, up, km, kp = U[p, at], U[p + 2, at], K[p, at], K[p + 2, at]
         su = yz(u) + (um + up)
         sku = yz(u * k) + (km * um + kp * up)
-        q = k[8 : R + 8]
-        return u[8 : R + 8], q, k, km + kp, 0.5 * (q * su + sku)
+        q = k[8 : size + 8]
+        return u[8 : size + 8], q, k, km + kp, 0.5 * (q * su + sku)
 
     def sweep_one(i, _):
-        p, start = i // CHUNKS, pl.multiple_of((i % CHUNKS) * R, R)
-        rows = pl.ds(start, R)
-        u, q, k, kx, near = nearby(U0, p, start)
+        p, start = i // (CHUNKS // 2), pl.multiple_of((i % (CHUNKS // 2)) * 2 * R, 2 * R)
+        rows = pl.ds(start, 2 * R)
+        u, q, k, kx, near = nearby(U0, p, start, 2 * R)
         d = 3.0 * q + 0.5 * (yz(k) + kx)
         total = src[p, rows] + near
         D[p, rows] = d
         N[p, rows] = total
-        U1[p + 1, pl.ds(start + 8, R)] = 0.2 * u + 0.8 * total / d
-        return 0
-
-    lax.fori_loop(0, 4 * CHUNKS, sweep_one, 0)
+        U1[p + 1, pl.ds(start + 8, 2 * R)] = 0.2 * u + 0.8 * total / d
+        return 0
+
+    lax.fori_loop(0, 2 * CHUNKS, sweep_one, 0)
 
     own[...] = to_coarse(
         my[...], mz, (K[1, 8 : ny + 8] + K[2, 8 : ny + 8]) + (K[3, 8 : ny + 8] + K[4, 8 : ny + 8])

time: 30.5 us -> 31.2 us (1.023)
  Pallas kernels: 29.7 us -> 30.5 us
    pallas_call x1, Pallas kernels: 25.5 us -> 26.3 us  [local(): pl.pallas_call(functools.partial(smooth_kernel, n, ny, nz), out_shape=(ja...]
where the time goes in v5:
time: 31.2 us; the launch traced here: 31.1 us
  Pallas kernels  30.5 us (98%)
  between operations  0.64 us (2%)
    pallas_call x1, Pallas kernels, local(): pl.pallas_call(functools.partial(smooth_kernel, n, ny, nz), out_shape=(ja...  26.3 us
    pallas_call x1, Pallas kernels, local(): pl.pallas_call(functools.partial(coarse_kernel, n, min(16, n)), out_shape...  4.19 us

profile of v5, /device:TPU:0, one launch (start us, length us, event | category | flops | bytes accessed | tf_op | source)
XLA Modules:
  0.0 31.1 jit_solution(5667521570801606226)
XLA Ops:
  0.6 26.3 %smooth.1 = (f32[4,128,256]{2,1,0:T(8,128)}, f32[16,16,128]{2,1,0:T(8,128)}, f32[6,16,16,128]{3,2,1,0:T(8,128)}, f32[16,16,128]{2,1,0:T(8,128)}) custom-call(f32[4,128,256]{2,1,0:T(8,128)} %source_hbm.1, f32[4,128,256]{2,1,0:T(8,128)} %guess_hbm.1, f32[4,128,256]{2,1,0:T(8,128)} %logq_hbm.1, bf16[32,128]{1,0:T(8,128)(2,1)} %constant.12.clone.ry_hbm, ...), custom_call_target="tpu_custom_call" | custom-call | tf_op jit(solution)/shard_map/smooth/pallas_call | solution.py:542
  26.9 4.2 %coarse.1 = (f32[4,128,256]{2,1,0:T(8,128)}, f32[1,2048]{1,0:T(1,128)}) custom-call(s32[16]{0:T(128)} %owner_hbm.1, f32[16,16,128]{2,1,0:T(8,128)} %get-tuple-element.6.rhs_hbm, f32[6,16,16,128]{3,2,1,0:T(8,128)} %get-tuple-element.7.coef_hbm, f32[16,16,128]{2,1,0:T(8,128)} %get-tuple-element.8.scaled_hbm, f32[4,128,256]{2,1,0:T(8,128)} %get-tuple-element.9.smooth_hbm, ...), custom_call_target="tpu_custom_call" | custom-call | tf_op jit(solution)/shard_map/coarse/pallas_call | solution.py:570
